TPU v7x, 32 devices: a whole 2x2x4 slice. The times are simulated.
32 devices in a mesh: groups: 2 (over y), row: 16 (over z, x, core).
Axes of the slice: x: 2, y: 2, z: 4, core: 2. Of those that a mesh axis runs over, the one named last changes fastest.
Arguments:
- strain_data: float32 [32, 32, 24576], P('row', None, 'groups'), parts along dimension 2, may hold values from -6 to 6
Outputs:
- coherence: float32 [2, 24576, 12288], P(None, ('groups', 'row')), parts along dimension 1
There are 2 independent parts, one for each index of `groups`. A program takes and returns all parts, laid end to end along the dimension named above; each array names one. Nothing has to cross between parts.
All inputs are finite; a program needn't handle non-finite values.
Results may differ from a plain program's by a relative error of at most 0.00008.
Values sent between devices are 32-bit elements; how exact they have to be, the bound alone decides.
A program may use at most 256 MiB of HBM per device.

v0:
```python
import jax
import jax.numpy as jnp
from jax import lax
from jax.sharding import PartitionSpec as P

FBIN = 5


def project(strain_data):
    samples = strain_data.shape[1]
    position = jnp.arange(samples, dtype=jnp.float32)
    taper = 0.5 - 0.5 * jnp.cos(2.0 * jnp.pi * (position + 0.5) / samples)
    phase = 2.0 * jnp.pi * FBIN * position / samples
    weights = jnp.stack([taper * jnp.cos(phase), -taper * jnp.sin(phase)])
    rms = jnp.sqrt(jnp.mean(strain_data * strain_data, axis=1, keepdims=True))
    normed = strain_data / jnp.maximum(rms, 1.0)
    return jnp.einsum("ks,psc->kpc", weights, normed, precision=lax.Precision.HIGHEST)


def cross(left, right):
    real_part = jnp.einsum(
        "pa,pb->ab", left[0], right[0], precision=lax.Precision.HIGHEST
    ) + jnp.einsum("pa,pb->ab", left[1], right[1], precision=lax.Precision.HIGHEST)
    imag_part = jnp.einsum(
        "pa,pb->ab", left[1], right[0], precision=lax.Precision.HIGHEST
    ) - jnp.einsum("pa,pb->ab", left[0], right[1], precision=lax.Precision.HIGHEST)
    return jnp.stack([real_part, imag_part])


def on_device(strain_data):
    spectrum = project(strain_data)
    channels = strain_data.shape[2]
    devices = lax.axis_size("row")
    width = channels // devices
    offset = lax.axis_index("row") * width
    gathered = lax.all_gather(spectrum, "row", axis=1, tiled=True)
    own_rows = lax.dynamic_slice_in_dim(gathered, offset, width, 2)
    scale = lax.rsqrt(jnp.sum(gathered * gathered, axis=(0, 1)) + 1e-06)
    own_scale = lax.dynamic_slice_in_dim(scale, offset, width, 0)
    coherence = cross(own_rows, gathered) * own_scale[None, :, None] * scale[None, None, :]
    return coherence


def solution(mesh):
    in_specs = (P("row", None, "groups"),)
    out_specs = P(None, ("groups", "row"), None)
    return jax.shard_map(
        on_device, mesh=mesh, in_specs=in_specs, out_specs=out_specs, check_vma=False
    )
```

profile of v0, /device:TPU:0, one launch (start us, length us, event | category | flops | bytes accessed | tf_op | source)
XLA Modules:
  0.0 262.5 jit_solution(7843653797047831028)
XLA Ops:
  6.5 0.0 copy-start.1
  6.5 0.0 all-gather.2.cloned.1.call-start
  6.5 0.1 fusion.26
  6.6 2.5 multiply_reduce_fusion.1
  9.1 0.1 sqrt_maximum_fusion
  9.2 0.2 copy-done.1
  9.4 2.4 fusion.1
  11.8 0.0 all-gather.2.cloned.1.call-update
  11.8 48.0 %all-gather.2.cloned.1.call-done = f32[2,32,12288]{2,0,1:T(2,128)} async-done(((f32[2,2,12288]{2,0,1:T(2,128)}), f32[2,32,12288]{2,0,1:T(2,128)}) %all-gather.2.cloned.1.call-update) | async-done | bytes 3145744 | tf_op jit(solution)/shard_map/all_gather | solution.py:36
  59.9 0.0 copy-start
  59.9 3.5 %multiply_reduce_fusion = f32[12288]{0:T(1024)S(1)} fusion(f32[2,32,12288]{2,0,1:T(2,128)} %all-gather.2.cloned.1.call-done), kind=kLoop, calls=%fused_computation.4 | loop fusion | flops 1560576 | bytes 3194880 | tf_op jit(solution)/shard_map/reduce_sum | solution.py:38
  63.3 0.1 dynamic_slice.7
  63.4 0.0 copy-done
  63.4 2.4 fusion.33
  65.9 0.3 constant_dynamic-slice_fusion
  66.1 34.2 %fusion.5 = f32[768,12288]{1,0:T(8,128)} fusion(f32[1,32,12288]{2,0,1:T(1,128)S(1)} %get-tuple-element.8, f32[1,32,768]{2,0,1:T(1,128)S(1)} %get-tuple-element.6), kind=kOutput, calls=%fused_computation.10 | convolution fusion | flops 3623878656 | bytes 39419904 | tf_op jit(solution)/shard_map/pa,pb->ab/dot_general | solution.py:24
  100.3 33.9 %fusion.7 = f32[768,12288]{1,0:T(8,128)} fusion(f32[1,32,12288]{2,0,1:T(1,128)S(1)} %get-tuple-element.8, f32[1,32,768]{2,0,1:T(1,128)S(1)} %get-tuple-element.5), kind=kOutput, calls=%fused_computation.12 | convolution fusion | flops 3623878656 | bytes 39419904 | tf_op jit(solution)/shard_map/pa,pb->ab/dot_general | solution.py:21
  134.2 36.2 %subtract_bitcast_fusion = f32[1,768,12288]{2,1,0:T(8,128)} fusion(f32[768,12288]{1,0:T(8,128)} %fusion.5, f32[1,32,12288]{2,0,1:T(1,128)S(1)} %get-tuple-element.7, f32[1,32,768]{2,0,1:T(1,128)S(1)} %get-tuple-element.5), kind=kOutput, calls=%fused_computation.2 | convolution fusion | flops 3633315840 | bytes 77168640 | tf_op jit(solution)/shard_map/pa,pb->ab/dot_general | solution.py:26
  170.4 36.3 %add_bitcast_fusion = f32[1,768,12288]{2,1,0:T(8,128)} fusion(f32[768,12288]{1,0:T(8,128)} %fusion.7, f32[1,32,12288]{2,0,1:T(1,128)S(1)} %get-tuple-element.7, f32[1,32,768]{2,0,1:T(1,128)S(1)} %get-tuple-element.6), kind=kOutput, calls=%fused_computation.3 | convolution fusion | flops 3633315840 | bytes 77168640 | tf_op jit(solution)/shard_map/pa,pb->ab/dot_general | solution.py:23
  206.7 49.0 %fusion = f32[2,768,12288]{2,1,0:T(8,128)} fusion(f32[1,768,12288]{2,1,0:T(8,128)} %subtract_bitcast_fusion, f32[1,768,12288]{2,1,0:T(8,128)} %add_bitcast_fusion, f32[12288]{0:T(1024)S(1)} %add_rsqrt_fusion, f32[768]{0:T(1024)S(1)} %dynamic_slice.7), kind=kLoop, calls=%fused_computation.1 | loop fusion | flops 56623104 | bytes 151047168 | tf_op jit(solution)/shard_map/mul | solution.py:40
  (1 shorter events, 0.0 us)
Async XLA Ops:
  6.5 2.8 %copy-start.1 = (f32[2,32,12288]{2,1,0:T(8,128)S(1)}, f32[2,32,12288]{2,1,0:T(8,128)}, u32[]{:S(2)}) copy-start(f32[2,32,12288]{2,1,0:T(8,128)} %param.1) | copy-start | bytes 9437188
  6.5 53.3 %all-gather.2.cloned.1.call-start = ((), (), s32[]{:S(2)}) async-start(), calls=%async_computation | async-start | bytes 3342336 | tf_op jit(solution)/shard_map/all_gather | solution.py:36
  59.9 3.6 %copy-start = (f32[2,32,12288]{2,0,1:T(2,128)S(1)}, f32[2,32,12288]{2,0,1:T(2,128)}, u32[]{:S(2)}) copy-start(f32[2,32,12288]{2,0,1:T(2,128)} %all-gather.2.cloned.1.call-done) | copy-start | bytes 9437188
Sparse Core Ops, SparseCore 0:
  11.9 47.8 all-gather.1
where the time goes:
time: 263 us
  matrix products  143 us (54%)
  other arithmetic  55.1 us (21%)
  waiting for transfers between devices  48.1 us (18%)
  between operations  13.4 us (5%)
  local copies, waits for them, and re-layouts  2.96 us (1%)
    mul x1, other arithmetic, on_device(): cross(own_rows, gathered) * own_scale[None, :, None] * scale[None, None, :]  49 us
    all_gather x1, waiting for transfers between devices, on_device(): gathered = lax.all_gather(spectrum, 'row', axis=1, tiled=True)  48 us
    dot_general x1, matrix products, cross(): jnp.einsum('pa,pb->ab', left[1], right[1], precision=lax.Precision.HIGHEST)  36.3 us
    dot_general x1, matrix products, cross(): jnp.einsum('pa,pb->ab', left[0], right[1], precision=lax.Precision.HIGHEST)  36.2 us
    dot_general x1, matrix products, cross(): jnp.einsum('pa,pb->ab', left[1], right[0], precision=lax.Precision.HIGHEST)  34.2 us
    dot_general x1, matrix products, cross(): jnp.einsum('pa,pb->ab', left[0], right[0], precision=lax.Precision.HIGHEST)  33.9 us
  transfers between devices with their start and end apart: 1, of which 1 were waited for; matrix products, arithmetic and copies ran while one was open for 0% of the time, Pallas kernels for 0%

commit v1 on v0

v1 whole, which is shorter than its diff:
```python
import jax
import jax.numpy as jnp
import numpy as np
from jax import lax
from jax.experimental import pallas as pl
from jax.experimental.pallas import tpu as pltpu
from jax.sharding import PartitionSpec as P

FBIN = 5


def divisor(size, largest):
    return max(w for w in range(128, largest + 1, 128) if size % w == 0)


def taper_weights(samples):
    position = np.arange(samples)
    taper = 0.5 - 0.5 * np.cos(2.0 * np.pi * (position + 0.5) / samples)
    phase = 2.0 * np.pi * FBIN * position / samples
    return np.stack([taper * np.cos(phase), -taper * np.sin(phase)]).astype(np.float32)


def project_kernel(weights_ref, strain_ref, out_ref):
    panes, samples, _ = strain_ref.shape
    for p in range(panes):
        x = strain_ref[p]
        rms = jnp.sqrt(jnp.sum(x * x, axis=0, keepdims=True) * (1.0 / samples))
        inverse = 1.0 / jnp.maximum(rms, 1.0)
        for k in range(2):
            total = jnp.sum(x * weights_ref[k], axis=0, keepdims=True) * inverse
            out_ref[0, pl.ds(k * panes + p, 1), :] = total


def project(strain):
    panes, samples, channels = strain.shape
    width = divisor(channels, 2048)
    weights = jnp.asarray(taper_weights(samples))[:, :, None]
    return pl.pallas_call(
        project_kernel,
        grid=(channels // width,),
        in_specs=[
            pl.BlockSpec((2, samples, 1), lambda j: (0, 0, 0)),
            pl.BlockSpec((panes, samples, width), lambda j: (0, 0, j)),
        ],
        out_specs=pl.BlockSpec((1, 2 * panes, width), lambda j: (0, 0, j)),
        out_shape=jax.ShapeDtypeStruct((1, 2 * panes, channels), jnp.float32),
    )(weights, strain)


def scaled(g):
    power = jnp.sum(g * g, axis=0, keepdims=True)
    return g * lax.rsqrt(power + 1e-06)


def halves(x):
    high = x.astype(jnp.bfloat16)
    return high, (x - high.astype(jnp.float32)).astype(jnp.bfloat16)


def cross_kernel(own_ref, all_ref, out_ref, left_ref):
    devices, rows, block = all_ref.shape
    depth = devices * rows
    panes = rows // 2

    @pl.when(pl.program_id(0) == 0)
    def _():
        own = scaled(own_ref[...].reshape(depth, own_ref.shape[2]))
        split = own.reshape(devices, rows, own.shape[1])
        turned = jnp.concatenate([split[:, panes:], -split[:, :panes]], axis=1)
        for part, u in enumerate((own, turned.reshape(own.shape))):
            high, low = halves(u.T)
            left_ref[part] = jnp.concatenate([high, low, high], axis=1)

    high, low = halves(scaled(all_ref[...].reshape(depth, block)))
    right = jnp.concatenate([high, high, low], axis=0)
    for part in range(2):
        out_ref[part] = jnp.dot(
            left_ref[part], right, preferred_element_type=jnp.float32
        )


def cross(own, gathered):
    devices, rows, channels = gathered.shape
    width = own.shape[2]
    block = divisor(channels, 512)
    depth = 3 * devices * rows
    return pl.pallas_call(
        cross_kernel,
        grid=(channels // block,),
        in_specs=[
            pl.BlockSpec((devices, rows, width), lambda j: (0, 0, 0)),
            pl.BlockSpec((devices, rows, block), lambda j: (0, 0, j)),
        ],
        out_specs=pl.BlockSpec((2, width, block), lambda j: (0, 0, j)),
        out_shape=jax.ShapeDtypeStruct((2, width, channels), jnp.float32),
        scratch_shapes=[pltpu.VMEM((2, width, depth), jnp.bfloat16)],
        compiler_params=pltpu.CompilerParams(vmem_limit_bytes=48 * 1024 * 1024),
    )(own, gathered)


def on_device(strain_data):
    channels = strain_data.shape[2]
    width = channels // lax.axis_size("row")
    offset = lax.axis_index("row") * width
    gathered = lax.all_gather(project(strain_data), "row", axis=0, tiled=True)
    own = lax.dynamic_slice_in_dim(gathered, offset, width, 2)
    return cross(own, gathered)


def solution(mesh):
    in_specs = (P("row", None, "groups"),)
    out_specs = P(None, ("groups", "row"), None)
    return jax.shard_map(
        on_device, mesh=mesh, in_specs=in_specs, out_specs=out_specs, check_vma=False
    )
```

time: 263 us -> 98.5 us (0.37)
  matrix products: 143 us -> 0 us
  other arithmetic: 55.1 us -> 0 us
  Pallas kernels: 0 us -> 33.9 us
    dot_general x5 -> x0, matrix products: 143 us -> none  [the longest x1 36.3 us: cross(): jnp.einsum('pa,pb->ab', left[1], right[1], precision=lax.Precision.HIGHEST)]
    mul x2 -> x0, other arithmetic: 49 us -> none  [the longest x1 49 us: on_device(): cross(own_rows, gathered) * own_scale[None, :, None] * scale[None, None, :]]
    pallas_call x0 -> x2, Pallas kernels: none -> 33.9 us  [the longest x1 28.7 us: cross(): pl.pallas_call(cross_kernel, grid=(channels // block,), in_specs=[pl.Bloc...]
    reduce_sum x2 -> x0, other arithmetic: 5.94 us -> none  [the longest x1 3.46 us: on_device(): scale = lax.rsqrt(jnp.sum(gathered * gathered, axis=(0, 1)) + 1e-06)]
    slice x2 -> x0, local copies, waits for them, and re-layouts: 2.71 us -> none  [the longest x1 2.43 us: cross(): right[1]]
where the time goes in v1:
time: 98.5 us; the launch traced here: 98.2 us
  waiting for transfers between devices  48.1 us (49%)
  Pallas kernels  33.9 us (34%)
  between operations  13.4 us (14%)
  local copies, waits for them, and re-layouts  2.82 us (3%)
    all_gather x1, waiting for transfers between devices, on_device(): gathered = lax.all_gather(project(strain_data), 'row', axis=0, tiled=True)  48 us
    pallas_call x1, Pallas kernels, cross(): pl.pallas_call(cross_kernel, grid=(channels // block,), in_specs=[pl.Bloc...  28.7 us
    pallas_call x1, Pallas kernels, project(): pl.pallas_call(project_kernel, grid=(channels // width,), in_specs=[pl.Bl...  5.24 us
  transfers between devices with their start and end apart: 1, of which 1 were waited for; matrix products, arithmetic and copies ran while one was open for 0% of the time, Pallas kernels for 0%

profile of v1, /device:TPU:0, one launch (start us, length us, event | category | flops | bytes accessed | tf_op | source)
XLA Modules:
  0.0 98.2 jit_solution(783769517695045768)
XLA Ops:
  6.5 0.0 all-gather.2.cloned.1.call-start
  6.5 5.2 %shard_map.28 = f32[1,4,12288]{2,1,0:T(4,128)} custom-call(f32[2,32,1]{2,1,0:T(8,128)} %constant.14.weights_ref, f32[2,32,12288]{2,1,0:T(8,128)} %strain_ref.1), custom_call_target="tpu_custom_call" | custom-call | tf_op jit(solution)/shard_map/pallas_call | solution.py:38
  11.8 0.0 all-gather.2.cloned.1.call-update
  11.8 48.0 %all-gather.2.cloned.1.call-done.all_ref = f32[16,4,12288]{2,1,0:T(4,128)} async-done(((f32[1,4,12288]{2,1,0:T(4,128)}), f32[16,4,12288]{2,1,0:T(4,128)}) %all-gather.2.cloned.1.call-update) | async-done | bytes 3145744 | tf_op jit(solution)/shard_map/all_gather | solution.py:105
  59.8 0.9 constant_dynamic-slice_fusion.own_ref
  60.8 0.0 copy-start
  60.8 1.9 %copy-done = f32[16,4,12288]{2,1,0:T(4,128)S(1)} copy-done((f32[16,4,12288]{2,1,0:T(4,128)S(1)}, f32[16,4,12288]{2,1,0:T(4,128)}, u32[]{:S(2)}) %copy-start) | copy-done | bytes 3145752
  62.7 28.7 %shard_map.29 = f32[2,768,12288]{2,1,0:T(8,128)} custom-call(f32[16,4,768]{2,1,0:T(4,128)S(1)} %constant_dynamic-slice_fusion.own_ref, f32[16,4,12288]{2,1,0:T(4,128)S(1)} %copy-done), custom_call_target="tpu_custom_call" | custom-call | tf_op jit(solution)/shard_map/pallas_call | solution.py:87
Async XLA Ops:
  6.5 53.3 %all-gather.2.cloned.1.call-start = ((), (), s32[]{:S(2)}) async-start(), calls=%async_computation | async-start | bytes 3342336 | tf_op jit(solution)/shard_map/all_gather | solution.py:105
  60.8 1.9 %copy-start = (f32[16,4,12288]{2,1,0:T(4,128)S(1)}, f32[16,4,12288]{2,1,0:T(4,128)}, u32[]{:S(2)}) copy-start(f32[16,4,12288]{2,1,0:T(4,128)} %all-gather.2.cloned.1.call-done.all_ref) | copy-start | bytes 9437188
Sparse Core Ops, SparseCore 0:
  11.9 47.8 all-gather.1

commit v2 on v1

--- a/solution.py
+++ b/solution.py
@@ -1,3 +1,5 @@
+import functools
+
 import jax
 import jax.numpy as jnp
 import numpy as np
@@ -45,6 +47,101 @@
         out_specs=pl.BlockSpec((1, 2 * panes, width), lambda j: (0, 0, j)),
         out_shape=jax.ShapeDtypeStruct((1, 2 * panes, channels), jnp.float32),
     )(weights, strain)
+
+
+def gather_kernel(devices, x_ref, out_ref, local_sem, ring_send, ring_recv, pair_send, pair_recv):
+    chips, half = devices // 2, devices // 4
+    columns = out_ref.shape[2] // 2
+    me = lax.axis_index("row")
+    core = me % 2
+    chip = me // 2
+    position = chip // 2 + (chip % 2) * (chips - 1 - 2 * (chip // 2))
+    sibling = me + 1 - 2 * core
+
+    def device_at(shift):
+        p = (position + chips + shift) % chips
+        back = p // half
+        return 2 * (2 * p + back * (2 * (chips - 1 - p) + 1 - 2 * p)) + core
+
+    def piece(ref, direction, last):
+        return ref.at[:, pl.ds(direction * columns, columns)] if last else ref
+
+    def ring_copy(direction, step):
+        ahead = 1 - 2 * direction
+        origin = device_at(-ahead * step)
+        source = x_ref.at[0] if step == 0 else out_ref.at[origin]
+        last = step == half - 1
+        return pltpu.make_async_remote_copy(
+            src_ref=piece(source, direction, last),
+            dst_ref=piece(out_ref.at[origin], direction, last),
+            send_sem=ring_send.at[2 * step + direction],
+            recv_sem=ring_recv.at[2 * step + direction],
+            device_id={"row": device_at(ahead)},
+            device_id_type=pl.DeviceIdType.MESH,
+        )
+
+    def pair_copy(direction, step):
+        ahead = 1 - 2 * direction
+        origin = device_at(-ahead * step)
+        block = piece(out_ref.at[origin], direction, step == half)
+        source = x_ref.at[0] if step == 0 else block
+        index = 2 * step + direction
+        return pltpu.make_async_remote_copy(
+            src_ref=source,
+            dst_ref=block,
+            send_sem=pair_send.at[index],
+            recv_sem=pair_recv.at[index],
+            device_id={"row": sibling},
+            device_id_type=pl.DeviceIdType.MESH,
+        )
+
+    barrier = pltpu.get_barrier_semaphore()
+    for partner in (device_at(1), device_at(-1), sibling):
+        pl.semaphore_signal(
+            barrier, inc=1, device_id={"row": partner}, device_id_type=pl.DeviceIdType.MESH
+        )
+    pl.semaphore_wait(barrier, 3)
+
+    ring = {(d, 0): ring_copy(d, 0) for d in range(2)}
+    for copy in ring.values():
+        copy.start()
+    own = pltpu.make_async_copy(x_ref.at[0], out_ref.at[me], local_sem)
+    own.start()
+    pairs = [pair_copy(0, 0)]
+    pairs[0].start()
+    for step in range(half):
+        for d in range(2):
+            ring[d, step].wait_recv()
+            if step + 1 < half:
+                ring[d, step + 1] = ring_copy(d, step + 1)
+                ring[d, step + 1].start()
+            pairs.append(pair_copy(d, step + 1))
+            pairs[-1].start()
+    own.wait()
+    for copy in ring.values():
+        copy.wait_send()
+    for copy in pairs:
+        copy.wait()
+
+
+def gather(spectrum):
+    devices = lax.axis_size("row")
+    _, rows, channels = spectrum.shape
+    copies = devices // 2
+    return pl.pallas_call(
+        functools.partial(gather_kernel, devices),
+        in_specs=[pl.BlockSpec(memory_space=pl.ANY)],
+        out_specs=pl.BlockSpec(memory_space=pl.ANY),
+        out_shape=jax.ShapeDtypeStruct((devices, rows, channels), jnp.float32),
+        scratch_shapes=[
+            pltpu.SemaphoreType.DMA,
+            pltpu.SemaphoreType.DMA((copies,)),
+            pltpu.SemaphoreType.DMA((copies,)),
+            pltpu.SemaphoreType.DMA((copies + 2,)),
+            pltpu.SemaphoreType.DMA((copies + 2,)),
+        ],
+        compiler_params=pltpu.CompilerParams(collective_id=0, has_side_effects=True),
+    )(spectrum)
 
 
 def scaled(g):
@@ -102,7 +199,7 @@
     channels = strain_data.shape[2]
     width = channels // lax.axis_size("row")
     offset = lax.axis_index("row") * width
-    gathered = lax.all_gather(project(strain_data), "row", axis=0, tiled=True)
+    gathered = gather(project(strain_data))
     own = lax.dynamic_slice_in_dim(gathered, offset, width, 2)
     return cross(own, gathered)
 

time: 98.5 us -> 65.3 us (0.66)
  waiting for transfers between devices: 48.1 us -> 0 us
  Pallas kernels: 33.9 us -> 62.2 us
  between operations: 13.4 us -> 0.02 us
    all_gather x1 -> x0, waiting for transfers between devices: 48 us -> none  [on_device(): gathered = lax.all_gather(project(strain_data), 'row', axis=0, tiled=True)]
    pallas_call x0 -> x1, Pallas kernels: none -> 28.2 us  [gather(): pl.pallas_call(functools.partial(gather_kernel, devices), in_specs=[pl.Bl...]
  transfers between devices with their start and end apart: 1 -> 0, of which waited for: 1 -> 0; matrix products, arithmetic and copies ran while one was open for 0% -> 0% of each run, Pallas kernels for 0% -> 0%
where the time goes in v2:
time: 65.3 us; the launch traced here: 65 us
  Pallas kernels  62.2 us (95%)
  local copies, waits for them, and re-layouts  2.83 us (4%)
    pallas_call x1, Pallas kernels, cross(): pl.pallas_call(cross_kernel, grid=(channels // block,), in_specs=[pl.Bloc...  28.7 us
    pallas_call x1, Pallas kernels, gather(): pl.pallas_call(functools.partial(gather_kernel, devices), in_specs=[pl.Bl...  28.2 us
    pallas_call x1, Pallas kernels, project(): pl.pallas_call(project_kernel, grid=(channels // width,), in_specs=[pl.Bl...  5.24 us
    unnamed x2, local copies, waits for them, and re-layouts  1.88 us

profile of v2, /device:TPU:0, one launch (start us, length us, event | category | flops | bytes accessed | tf_op | source)
XLA Modules:
  0.0 65.0 jit_solution(14381586110275584822)
XLA Ops:
  0.0 5.2 %shard_map.28.x_ref = f32[1,4,12288]{2,1,0:T(4,128)} custom-call(f32[2,32,1]{2,1,0:T(8,128)} %constant.14.weights_ref, f32[2,32,12288]{2,1,0:T(8,128)} %strain_ref.1), custom_call_target="tpu_custom_call" | custom-call | tf_op jit(solution)/shard_map/pallas_call | solution.py:40
  5.2 28.2 %shard_map.29.all_ref = f32[16,4,12288]{2,1,0:T(4,128)} custom-call(f32[1,4,12288]{2,1,0:T(4,128)} %shard_map.28.x_ref), custom_call_target="tpu_custom_call" | custom-call | tf_op jit(solution)/shard_map/pallas_call | solution.py:131
  33.5 0.9 %constant_dynamic-slice_fusion.own_ref = f32[16,4,768]{2,1,0:T(4,128)S(1)} fusion(f32[16,4,12288]{2,1,0:T(4,128)} %shard_map.29.all_ref, s32[]{:T(128)S(6)} %select_n.3), kind=kLoop, calls=%fused_computation | loop fusion | bytes 393220 | tf_op jit(solution)/shard_map/dynamic_slice | solution.py:203
  34.4 0.0 copy-start
  34.4 1.9 %copy-done = f32[16,4,12288]{2,1,0:T(4,128)S(1)} copy-done((f32[16,4,12288]{2,1,0:T(4,128)S(1)}, f32[16,4,12288]{2,1,0:T(4,128)}, u32[]{:S(2)}) %copy-start) | copy-done | bytes 3145752
  36.3 28.7 %shard_map.30 = f32[2,768,12288]{2,1,0:T(8,128)} custom-call(f32[16,4,768]{2,1,0:T(4,128)S(1)} %constant_dynamic-slice_fusion.own_ref, f32[16,4,12288]{2,1,0:T(4,128)S(1)} %copy-done), custom_call_target="tpu_custom_call" | custom-call | tf_op jit(solution)/shard_map/pallas_call | solution.py:184
Async XLA Ops:
  34.4 1.9 %copy-start = (f32[16,4,12288]{2,1,0:T(4,128)S(1)}, f32[16,4,12288]{2,1,0:T(4,128)}, u32[]{:S(2)}) copy-start(f32[16,4,12288]{2,1,0:T(4,128)} %shard_map.29.all_ref) | copy-start | bytes 9437188
